TPU v7x, 256 devices: a whole 4x4x8 slice. The times are simulated.
256 devices in a mesh: rep: 16 (over x_lo, z), fsdp: 16 (over x_hi, y, core).
Axes of the slice: x: 4 (x_hi: 2, x_lo: 2; x = x_hi * 2 + x_lo), y: 4, z: 8, core: 2. Of those that a mesh axis runs over, the one named last changes fastest.
Arguments:
- activations: bfloat16 [16, 2048, 8192], P('rep', 'fsdp'), may hold values from -6 to 6
- cotangent: bfloat16 [16, 2048, 1024], P('rep', 'fsdp'), may hold values from -0.013671875 to 0.013671875
- momentum: float32 [16, 8192, 1024], P('rep', 'fsdp'), may hold values from -6 to 6
- positions: int32 [16, 2048, 32], P('rep', 'fsdp'), may hold values from 0 to 4095, as said below
Outputs:
- new_momentum: float32 [16, 8192, 1024], P('rep', 'fsdp')
- step: float32 [8192, 1024], P('fsdp')
Inputs may be any that keep to these rules, and one draw needn't show every extreme that they name: Within one replica and one group the 32 positions are distinct.
All inputs are finite; a program needn't handle non-finite values.
Results may differ from a plain program's by a relative error of at most 0.0017.
Values may be sent and summed in bfloat16 or wider, within the bound.
A program may use at most 128 MiB of HBM per device.

v0:
```python
import jax
import jax.numpy as jnp
from jax import lax
from jax.sharding import PartitionSpec as P

GROUP = 64


momentum_decay = 0.999
sharpness = 4.0


def dct_table(extent):
    frequency = jnp.arange(extent, dtype=jnp.float32)[:, None]
    location = jnp.arange(extent, dtype=jnp.float32)[None, :]
    cosines = jnp.cos(jnp.pi * (2.0 * location + 1.0) * frequency / (2.0 * extent)) * jnp.sqrt(
        2.0 / extent
    )
    return jnp.where(frequency == 0.0, cosines * jnp.sqrt(0.5), cosines)


def forward_dct(spatial, cosines):
    row_count, col_count = spatial.shape
    extent = cosines.shape[0]
    blocks = spatial.reshape(row_count // extent, extent, col_count // extent, extent)
    coeffs = jnp.einsum(
        "hi,piqj,lj->hlpq", cosines, blocks, cosines, precision=lax.Precision.HIGHEST
    )
    return coeffs.reshape(extent, extent, -1)


def inverse_dct(coeffs, cosines, row_count, col_count):
    extent = cosines.shape[0]
    grid_form = coeffs.reshape(extent, extent, row_count // extent, col_count // extent)
    spatial = jnp.einsum(
        "hi,hlpq,lj->piqj", cosines, grid_form, cosines, precision=lax.Precision.HIGHEST
    )
    return spatial.reshape(row_count, col_count)


def one_hots(spot_list, extent):
    levels = jnp.arange(extent, dtype=jnp.int32)[:, None]
    expanded = spot_list[..., None, :]
    upper_hot = (expanded // extent == levels).astype(jnp.float32)
    lower_hot = (expanded % extent == levels).astype(jnp.float32)
    return (upper_hot, lower_hot)


def per_device(activations, cotangent, momentum, positions):
    tokens = activations[0]
    upstream = cotangent[0]
    moment = momentum[0]
    row_count, col_count = moment.shape
    cosines = dct_table(GROUP)
    gradient = lax.psum_scatter(
        lax.dot_general(
            tokens, upstream, (((0,), (0,)), ((), ())), preferred_element_type=jnp.float32
        ).astype(jnp.bfloat16),
        "fsdp",
        scatter_dimension=0,
        tiled=True,
    ).astype(jnp.float32)
    updated = momentum_decay * moment + gradient
    coeffs = forward_dct(updated, cosines)
    spot_list = positions[0].T
    upper_hot, lower_hot = one_hots(spot_list, GROUP)
    picked = jnp.einsum("hln,jhn->jln", coeffs, upper_hot, precision=lax.Precision.HIGHEST)
    values = jnp.sum(picked * lower_hot, axis=1)
    own_groups = jnp.einsum(
        "jhn,jln->hln", upper_hot * values[:, None, :], lower_hot, precision=lax.Precision.HIGHEST
    )
    next_moment = updated - inverse_dct(own_groups, cosines, row_count, col_count)
    part_values = lax.all_gather(values[None], "rep", axis=0, tiled=True)
    part_spots = lax.all_gather(spot_list[None], "rep", axis=0, tiled=True)
    upper_all, lower_all = one_hots(part_spots, GROUP)
    dense_sum = jnp.einsum(
        "kjhn,kjln->hln",
        upper_all * part_values[:, :, None, :],
        lower_all,
        precision=lax.Precision.HIGHEST,
    )
    update = inverse_dct(dense_sum, cosines, row_count, col_count)
    return (next_moment[None], jnp.tanh(sharpness * update))


def solution(mesh):
    return jax.shard_map(
        per_device,
        mesh=mesh,
        in_specs=(
            P("rep", "fsdp", None),
            P("rep", "fsdp", None),
            P("rep", "fsdp", None),
            P("rep", "fsdp", None),
        ),
        out_specs=(P("rep", "fsdp", None), P("fsdp", None)),
        check_vma=False,
    )
```

profile of v0, /device:TPU:2, one launch (start us, length us, event | category | flops | bytes accessed | tf_op | source)
XLA Modules:
  0.0 369.4 jit_solution(676404131417073263)
XLA Ops:
  7.2 0.0 copy-start
  7.2 0.0 reduce-scatter.2.cloned.1.call-start
  7.2 1.5 copy-done
  8.8 9.0 %convolution_convert_fusion = bf16[8192,1024]{1,0:T(8,128)(2,1)} fusion(bf16[1,128,8192]{2,1,0:T(8,128)(2,1)S(1)} %copy-done, bf16[1,128,1024]{2,1,0:T(8,128)(2,1)} %param.5), kind=kOutput, calls=%fused_computation.8 | convolution fusion | flops 2155872256 | bytes 19136512 | tf_op jit(solution)/shard_map/dot_general | solution.py:56
  17.8 0.0 copy-start.3
  17.8 0.0 reduce-scatter.2.cloned.1.call-update
  17.8 0.7 copy-done.3
  18.5 0.1 copy.31
  18.6 0.1 copy.32
  18.7 37.3 %all-gather = s32[512,128]{1,0:T(8,128)S(1)} all-gather(s32[32,128]{1,0:T(8,128)S(1)} %bitcast.68), channel_id=2, replica_groups=mesh['rep'=16,'fsdp'=16] {'rep'}, dimensions={0}, use_global_device_ids=true | all-gather | bytes 278528 | tf_op jit(solution)/shard_map/all_gather | solution.py:74
  56.0 0.2 add_select_fusion.1
  56.2 0.5 copy.37
  56.7 1.4 copy.38
  58.1 116.5 %reduce-scatter.2.cloned.1.call-done = bf16[512,1024]{1,0:T(8,128)(2,1)} async-done(((bf16[8192,1024]{1,0:T(8,128)(2,1)}), bf16[512,1024]{1,0:T(8,128)(2,1)}) %reduce-scatter.2.cloned.1.call-update) | async-done | bytes 1048592 | tf_op jit(solution)/shard_map/reduce_scatter | solution.py:55
  174.6 2.4 bitcast_add_fusion
  177.0 2.5 reshape.93
  179.6 7.4 %fusion.6 = f32[8,16,64,64]{2,3,1,0:T(8,128)S(1)} fusion(f32[8,64,16,64]{3,2,1,0:T(8,128)} %reshape.93, f32[64]{0:T(128)S(1)} %add_multiply_fusion, pred[64]{0:T(512)(128)(4,1)S(1)} %iota_compare_fusion.11), kind=kOutput, calls=%fused_computation.9 | convolution fusion | flops 402673664 | bytes 4194624 | tf_op jit(solution)/shard_map/hi,piqj,lj->hlpq/dot_general | solution.py:26
  187.0 3.9 %fusion.27 = f32[8,16,64,64]{3,2,1,0:T(8,128)S(1)} fusion(f32[8,16,64,64]{2,3,1,0:T(8,128)S(1)} %fusion.6, f32[64]{0:T(128)S(1)} %add_multiply_fusion, pred[64]{0:T(512)(128)(4,1)S(1)} %iota_compare_fusion.11), kind=kOutput, calls=%fused_computation.43 | convolution fusion | flops 402673664 | bytes 4194624 | tf_op jit(solution)/shard_map/hi,piqj,lj->hlpq/dot_general | solution.py:26
  190.9 3.1 fusion.8
  194.0 0.1 copy.39
  194.1 7.6 %fusion.10 = f32[128,64,64]{2,1,0:T(8,128)} fusion(f32[32,128]{0,1:T(8,128)S(1)} %fusion.8, s32[32,128]{0,1:T(8,128)S(1)} %copy.32, s32[32,128]{0,1:T(8,128)S(1)} %copy.31), kind=kOutput, calls=%fused_computation.18 | convolution fusion | flops 202113024 | bytes 2146304 | tf_op jit(solution)/shard_map/jhn,jln->hln/dot_general | solution.py:69
  201.7 35.4 %all-gather.1 = f32[512,128]{1,0:T(8,128)S(1)} all-gather(f32[32,128]{1,0:T(8,128)S(1)} %copy.39), channel_id=3, replica_groups=mesh['rep'=16,'fsdp'=16] {'rep'}, dimensions={0}, use_global_device_ids=true | all-gather | bytes 278528 | tf_op jit(solution)/shard_map/all_gather | solution.py:73
  237.1 1.4 copy.40
  238.5 14.0 %fusion.25 = f32[64,8,16,64]{0,3,2,1:T(8,128)S(1)} fusion(f32[64,64,8,16]{0,1,3,2:T(8,128)} %bitcast.64, f32[64]{0:T(128)S(1)} %add_multiply_fusion, pred[64]{0:T(512)(128)(4,1)S(1)} %iota_compare_fusion.11), kind=kOutput, calls=%fused_computation.41 | convolution fusion | flops 402673664 | bytes 4194624 | tf_op jit(solution)/shard_map/hi,hlpq,lj->piqj/dot_general | solution.py:35
  252.5 3.5 convolution_bitcast_fusion
  256.0 4.3 %copy.36 = f32[8,64,16,64]{3,2,1,0:T(8,128)} copy(f32[8,64,16,64]{3,1,2,0:T(8,128)S(1)} %convolution_bitcast_fusion) | data formatting | bytes 4194304 | tf_op jit(solution)/shard_map/hi,hlpq,lj->piqj/transpose | solution.py:35
  260.3 4.8 %reshape.96 = f32[512,1024]{1,0:T(8,128)} reshape(f32[8,64,16,64]{3,2,1,0:T(8,128)} %copy.36) | data formatting | bytes 4194304 | tf_op jit(solution)/shard_map/reshape | solution.py:38
  265.2 0.0 copy-start.2
  265.2 3.6 subtract_bitcast_fusion
  268.7 0.0 copy-done.2
  268.7 18.8 %fusion.91 = f32[16,32,64,128]{2,1,0,3:T(8,128)S(1)} fusion(f32[16,32,128]{1,0,2:T(8,128)} %copy.40, s32[16,32,128]{1,0,2:T(8,128)S(1)} %copy-done.2), kind=kLoop, calls=%fused_computation.1.clone.2 | loop fusion | flops 8388608 | bytes 17301504 | tf_op jit(solution)/shard_map/kjhn,kjln->hln/dot_general | solution.py:76
  287.5 49.4 %fusion = f32[128,64,64,1]{2,1,3,0:T(8,128)S(1)} fusion(s32[16,32,128]{1,0,2:T(8,128)S(1)} %copy.37, f32[16,32,64,128]{2,1,0,3:T(8,128)S(1)} %fusion.91), kind=kOutput, calls=%fused_computation | convolution fusion | flops 3225419776 | bytes 19136512 | tf_op jit(solution)/shard_map/kjhn,kjln->hln/dot_general | solution.py:76
  336.9 12.2 %fusion.22 = f32[64,8,16,64]{0,3,2,1:T(8,128)S(1)} fusion(f32[64,64,8,16]{0,1,3,2:T(8,128)S(1)} %bitcast.63, f32[64]{0:T(128)S(1)} %add_multiply_fusion, pred[64]{0:T(512)(128)(4,1)S(1)} %iota_compare_fusion.11), kind=kOutput, calls=%fused_computation.38 | convolution fusion | flops 402673664 | bytes 4194624 | tf_op jit(solution)/shard_map/hi,hlpq,lj->piqj/dot_general | solution.py:35
  349.1 3.7 tanh_bitcast_fusion
  352.8 0.0 copy-start.1
  352.8 4.6 %copy.42 = f32[8,64,16,64]{3,2,1,0:T(8,128)} copy(f32[8,64,16,64]{3,1,2,0:T(8,128)S(1)} %tanh_bitcast_fusion) | data formatting | bytes 4194304 | tf_op jit(solution)/shard_map/tanh | solution.py:83
  357.4 4.8 %tanh.11 = f32[512,1024]{1,0:T(8,128)} reshape(f32[8,64,16,64]{3,2,1,0:T(8,128)} %copy.42) | data formatting | bytes 4194304 | tf_op jit(solution)/shard_map/tanh | solution.py:83
  362.3 0.0 copy-done.1
  (3 shorter events, 0.0 us)
Async XLA Ops:
  7.2 1.6 copy-start
  7.2 167.4 %reduce-scatter.2.cloned.1.call-start = ((), (), s32[]{:S(2)}) async-start(), calls=%async_computation.1 | async-start | bytes 17825792 | tf_op jit(solution)/shard_map/reduce_scatter | solution.py:55
  17.8 0.7 copy-start.3
  265.2 3.6 copy-start.2
  352.8 9.4 %copy-start.1 = (bf16[1,128,8192]{2,1,0:T(8,128)(2,1)S(1)}, bf16[1,128,8192]{2,1,0:T(8,128)(2,1)}, u32[]{:S(2)}) copy-start(bf16[1,128,8192]{2,1,0:T(8,128)(2,1)} %param.4) | copy-start | bytes 6291460
Sparse Core Ops, SparseCore 0:
  18.0 156.6 reduce-scatter.1
where the time goes:
time: 372 us; the launch traced here: 369 us
  waiting for transfers between devices  117 us (31%)
  matrix products  114 us (31%)
  blocking collectives  72.7 us (20%)
  local copies, waits for them, and re-layouts  26.8 us (7%)
  other arithmetic  25 us (7%)
  between operations  14.4 us (4%)
    reduce_scatter x1, waiting for transfers between devices, per_device(): lax.psum_scatter(lax.dot_general(tokens, upstream, (((0,), (0,)), ((), ()...  116 us
    dot_general x1, matrix products, per_device(): jnp.einsum('kjhn,kjln->hln', upper_all * part_values[:, :, None, :], lowe...  49.4 us
    all_gather x1, blocking collectives, per_device(): part_spots = lax.all_gather(spot_list[None], 'rep', axis=0, tiled=True)  37.3 us
    all_gather x1, blocking collectives, per_device(): part_values = lax.all_gather(values[None], 'rep', axis=0, tiled=True)  35.4 us
    dot_general x4, matrix products, inverse_dct(): jnp.einsum('hi,hlpq,lj->piqj', cosines, grid_form, cosines, precision=lax...  33.4 us
    dot_general x1, other arithmetic, per_device(): jnp.einsum('kjhn,kjln->hln', upper_all * part_values[:, :, None, :], lowe...  18.8 us
    dot_general x2, matrix products, forward_dct(): jnp.einsum('hi,piqj,lj->hlpq', cosines, blocks, cosines, precision=lax.Pr...  11.3 us
    tanh x2, local copies, waits for them, and re-layouts, per_device(): return (next_moment[None], jnp.tanh(sharpness * update))  9.41 us
  transfers between devices with their start and end apart: 1, of which 1 were waited for; matrix products, arithmetic and copies ran while one was open for 1% of the time, Pallas kernels for 0%

commit v1 on v0

v1 whole, which is shorter than its diff:
```python
import functools

import jax
import jax.numpy as jnp
import numpy as np
from jax import lax
from jax.experimental import pallas as pl
from jax.experimental.pallas import tpu as pltpu
from jax.sharding import PartitionSpec as P

GROUP = 64
MESH = pl.DeviceIdType.MESH
BF = jnp.bfloat16
F32 = jnp.float32
NEAR = ((1, 0), (3, 0), (2, 0), (1, 1), (3, 1), (2, 1), (0, 1))


def dct_table():
    k = np.arange(GROUP, dtype=np.float64)[:, None]
    n = np.arange(GROUP, dtype=np.float64)[None, :]
    table = np.cos(np.pi * (2.0 * n + 1.0) * k / (2.0 * GROUP)) * np.sqrt(2.0 / GROUP)
    table[0] *= np.sqrt(0.5)
    return table


def split_const(a):
    hi = a.astype(np.float32).astype(jnp.bfloat16)
    lo = (a - hi.astype(np.float64)).astype(np.float32).astype(jnp.bfloat16)
    return hi, lo


def tables(left, right):
    rhi, rlo = split_const(np.kron(np.eye(4), right))
    lhi, llo = split_const(np.kron(np.eye(2), left))
    return np.concatenate([rhi, rlo], 0), np.concatenate([lhi, llo, lhi], 1)


def dot(a, b):
    return jnp.dot(a, b, preferred_element_type=F32)


def split(x):
    hi = x.astype(BF)
    return hi, (x - hi.astype(F32)).astype(BF)


def right_mul(x, table_ref):
    m = x.shape[0]
    hi, lo = split(x)
    both = dot(jnp.concatenate([hi, lo], 0), table_ref[0:256, :])
    return both[:m] + both[m:] + dot(hi, table_ref[256:512, :])


def left_mul(table_ref, y):
    hi, lo = split(y)
    return dot(table_ref[...], jnp.concatenate([hi, hi, lo], 0))


def one_hots(row):
    lane = lax.broadcasted_iota(jnp.int32, (1, 128), 1)
    target = (row & 63) + (lane // 32) * 64
    wide = lax.broadcasted_iota(jnp.int32, (256, 128), 0) == target
    high = lax.broadcasted_iota(jnp.int32, (64, 128), 0) == (row >> 6)
    return wide, high


def gather_kernel(
    act, cot, mom, pos, rtab, ltab,
    upd, vall, pall,
    abuf, cbuf, xsend, xrecv, mbuf,
    c_send, c_recv, f_send, f_recv, a_send, a_recv, x_send, x_recv,
    p_send, p_recv, v_send, v_recv, local,
):
    f = lax.axis_index("fsdp")
    r = lax.axis_index("rep")
    xh, y, c = f // 8, (f // 2) % 4, f % 2
    slot = y * 2 + c

    def near(dy, dc):
        return (y + dy) % 4, (c + dc) % 2

    def fs(xx, yy, cc):
        return {"fsdp": xx * 8 + yy * 2 + cc}

    def columns(xx, s, j):
        return pl.ds(pl.multiple_of((xx * 8 + s) * 512 + j * 128, 128), 128)

    def block(s):
        return pl.ds(pl.multiple_of(s * 128, 128), 128)

    def own_copy(j):
        xx = jnp.where(j < 4, 1 - xh, xh)
        return pltpu.make_async_copy(
            act.at[:, columns(xx, slot, j % 4)], abuf.at[j, block(slot)], local.at[j]
        )

    cot_copy = pltpu.make_async_copy(cot, cbuf.at[block(slot)], local.at[8])
    mom_copy = pltpu.make_async_copy(mom, mbuf, local.at[9])
    cot_copy.start()
    for j in range(8):
        own_copy(j).start()
    mom_copy.start()

    barrier = pltpu.get_barrier_semaphore()
    for dy, dc in NEAR:
        yy, cc = near(dy, dc)
        pl.semaphore_signal(barrier, inc=1, device_id=fs(xh, yy, cc), device_id_type=MESH)
    pl.semaphore_signal(barrier, inc=1, device_id=fs(1 - xh, y, c), device_id_type=MESH)
    for d in range(1, 16):
        pl.semaphore_signal(barrier, inc=1, device_id={"rep": (r + d) % 16}, device_id_type=MESH)
    pl.semaphore_wait(barrier, 23)

    def cot_send(i, dy, dc):
        yy, cc = near(dy, dc)
        return pltpu.make_async_remote_copy(
            src_ref=cot, dst_ref=cbuf.at[block(slot)], send_sem=c_send.at[i], recv_sem=c_recv.at[i],
            device_id=fs(xh, yy, cc), device_id_type=MESH,
        )

    def cot_arrival(i, dy, dc):
        yy, cc = near(4 - dy, dc)
        s = yy * 2 + cc
        return pltpu.make_async_remote_copy(
            src_ref=cbuf.at[block(s)], dst_ref=cbuf.at[block(s)], send_sem=c_send.at[i],
            recv_sem=c_recv.at[i], device_id=fs(xh, y, 1 - c), device_id_type=MESH,
        )

    def cot_forward(i, dy):
        s = ((y + 4 - dy) % 4) * 2 + c
        return pltpu.make_async_remote_copy(
            src_ref=cbuf.at[block(s)], dst_ref=cbuf.at[block(s)], send_sem=f_send.at[i],
            recv_sem=f_recv.at[i], device_id=fs(xh, y, 1 - c), device_id_type=MESH,
        )

    def act_send(i, dy, dc, j):
        yy, cc = near(dy, dc)
        xx = jnp.where(j < 4, 1 - xh, xh)
        return pltpu.make_async_remote_copy(
            src_ref=act.at[:, columns(xx, yy * 2 + cc, j % 4)], dst_ref=abuf.at[j, block(slot)],
            send_sem=a_send.at[i, j], recv_sem=a_recv.at[i, j],
            device_id=fs(xh, yy, cc), device_id_type=MESH,
        )

    def act_arrival(i, dy, dc, j):
        yy, cc = near(4 - dy, dc)
        s = yy * 2 + cc
        return pltpu.make_async_remote_copy(
            src_ref=abuf.at[j, block(s)], dst_ref=abuf.at[j, block(s)], send_sem=a_send.at[i, j],
            recv_sem=a_recv.at[i, j], device_id=fs(xh, y, 1 - c), device_id_type=MESH,
        )

    def part_send(j):
        return pltpu.make_async_remote_copy(
            src_ref=xsend.at[block(j)], dst_ref=xrecv.at[block(j)], send_sem=x_send.at[j],
            recv_sem=x_recv.at[j], device_id=fs(1 - xh, y, c), device_id_type=MESH,
        )

    def pos_send(d, source):
        return pltpu.make_async_remote_copy(
            src_ref=pos, dst_ref=pall.at[source], send_sem=p_send.at[d - 1], recv_sem=p_recv.at[d - 1],
            device_id={"rep": (r + d) % 16}, device_id_type=MESH,
        )

    def val_send(d, j, source):
        rows = pl.ds(pl.multiple_of(j * 8, 8), 8)
        return pltpu.make_async_remote_copy(
            src_ref=vall.at[source, rows], dst_ref=vall.at[source, rows], send_sem=v_send.at[d - 1, j],
            recv_sem=v_recv.at[d - 1, j], device_id={"rep": (r + d) % 16}, device_id_type=MESH,
        )

    with_mate = NEAR[:3] + NEAR[6:]
    for i, (dy, dc) in enumerate(with_mate):
        cot_send(i, dy, dc).start()

    def send_acts(j, carry):
        for i, (dy, dc) in enumerate(NEAR):
            act_send(i, dy, dc, j).start()
        return carry

    lax.fori_loop(0, 8, send_acts, 0)
    for d in range(1, 16):
        pos_send(d, r).start()
    pall[r] = pos[...]

    for i, (dy, dc) in enumerate(with_mate):
        cot_arrival(i, dy, dc).wait_recv()
        if i < 3:
            cot_forward(i, dy).start()
    for i, (dy, dc) in enumerate(NEAR[:3]):
        s = ((y + 4 - dy) % 4) * 2 + (1 - c)
        pltpu.make_async_remote_copy(
            src_ref=cbuf.at[block(s)], dst_ref=cbuf.at[block(s)], send_sem=f_send.at[i],
            recv_sem=f_recv.at[i], device_id=fs(xh, y, 1 - c), device_id_type=MESH,
        ).wait_recv()
    cot_copy.wait()

    def product(j):
        own_copy(j).wait()
        for i, (dy, dc) in enumerate(NEAR):
            act_arrival(i, dy, dc, j).wait_recv()
        return lax.dot_general(
            abuf[j], cbuf[...], (((0,), (0,)), ((), ())), preferred_element_type=F32
        )

    def partner(j, carry):
        xsend[block(j)] = product(j).astype(BF)
        part_send(j).start()
        return carry

    lax.fori_loop(0, 4, partner, 0)
    mom_copy.wait()

    def own(j, carry):
        grad = product(j + 4)
        part_send(j).wait_recv()
        rows = block(j)
        upd[rows] = 0.999 * mbuf[rows] + (grad + xrecv[rows].astype(F32))

        def chunk(q, inner):
            cols = pl.ds(pl.multiple_of(q * 256, 256), 256)
            coeffs = left_mul(ltab, right_mul(upd[rows, cols], rtab))
            for p in range(2):
                t = j * 8 + p * 4 + q
                wide, high = one_hots(pos[pl.ds(t, 1), :])
                hi, lo = split(coeffs[p * 64 : p * 64 + 64])
                both = dot(jnp.concatenate([hi, lo], 0), wide.astype(F32).astype(BF))
                picked = jnp.where(high, both[:64] + both[64:], 0.0)
                vall[r, pl.ds(t, 1), :] = jnp.sum(picked, axis=0, keepdims=True)
            return inner

        lax.fori_loop(0, 4, chunk, 0)
        for d in range(1, 16):
            val_send(d, j, r).start()
        return carry

    lax.fori_loop(0, 4, own, 0)

    def last(j, carry):
        for d in range(1, 16):
            val_send(d, j, (r + 16 - d) % 16).wait_recv()
            val_send(d, j, r).wait_send()
        part_send(j).wait_send()
        return carry

    lax.fori_loop(0, 4, last, 0)
    for d in range(1, 16):
        pos_send(d, (r + 16 - d) % 16).wait_recv()
        pos_send(d, r).wait_send()
    for i, (dy, dc) in enumerate(with_mate):
        cot_send(i, dy, dc).wait_send()
    for i in range(3):
        cot_forward(i, NEAR[i][0]).wait_send()

    def sent(j, carry):
        for i, (dy, dc) in enumerate(NEAR):
            act_send(i, dy, dc, j).wait_send()
        return carry

    lax.fori_loop(0, 8, sent, 0)


def spread_kernel(upd, vall, pall, vown, pown, rtab, ltab, nm, st, dense):
    def masks(row, val):
        wide, high = one_hots(row)
        hi = val.astype(BF).astype(F32)
        weights = jnp.concatenate([jnp.where(high, hi, 0.0), jnp.where(high, val - hi, 0.0)], 0)
        return weights.astype(BF), wide.astype(F32).astype(BF)

    def scatter(pairs):
        w = jnp.concatenate([a for a, _ in pairs], 1)
        z = jnp.concatenate([b for _, b in pairs], 1)
        both = lax.dot_general(w, z, (((1,), (1,)), ((), ())), preferred_element_type=F32)
        return both[:64] + both[64:]

    def tile(t, carry):
        one = pl.ds(t, 1)
        cols = pl.ds(pl.multiple_of((t % 4) * 256, 256), 256)
        rows = pl.multiple_of((t // 4) * 64, 64)
        dense[pl.ds(rows, 64), cols] = scatter(
            [masks(pall[k, one, :], vall[k, one, :]) for k in range(16)]
        )
        dense[pl.ds(128 + rows, 64), cols] = scatter([masks(pown[one, :], vown[one, :])])
        return carry

    lax.fori_loop(0, 8, tile, 0)

    def chunk(q, carry):
        cols = pl.ds(pl.multiple_of(q * 256, 256), 256)
        half = right_mul(dense[:, cols], rtab)
        st[:, cols] = jnp.tanh(4.0 * left_mul(ltab, half[:128]))
        nm[:, cols] = upd[:, cols] - left_mul(ltab, half[128:])
        return carry

    lax.fori_loop(0, 4, chunk, 0)


def per_device(activations, cotangent, momentum, positions):
    b = dct_table()
    f_right, f_left = (jnp.asarray(a) for a in tables(b, b.T))
    i_right, i_left = (jnp.asarray(a) for a in tables(b.T, b))
    pos = positions.reshape(32, 128)
    vmem = pl.BlockSpec(memory_space=pltpu.VMEM)
    hbm = pl.BlockSpec(memory_space=pl.ANY)
    dma = pltpu.SemaphoreType.DMA
    upd, vall, pall = pl.pallas_call(
        gather_kernel,
        out_shape=(
            jax.ShapeDtypeStruct((512, 1024), F32),
            jax.ShapeDtypeStruct((16, 32, 128), F32),
            jax.ShapeDtypeStruct((16, 32, 128), jnp.int32),
        ),
        in_specs=[hbm, hbm, hbm, vmem, vmem, vmem],
        out_specs=(vmem, vmem, vmem),
        scratch_shapes=[
            pltpu.VMEM((8, 1024, 128), BF),
            pltpu.VMEM((1024, 1024), BF),
            pltpu.VMEM((512, 1024), BF),
            pltpu.VMEM((512, 1024), BF),
            pltpu.VMEM((512, 1024), F32),
            dma((4,)), dma((4,)), dma((3,)), dma((3,)), dma((7, 8)), dma((7, 8)), dma((4,)), dma((4,)),
            dma((15,)), dma((15,)), dma((15, 4)), dma((15, 4)), dma((10,)),
        ],
        name="gather",
        compiler_params=pltpu.CompilerParams(
            collective_id=0, has_side_effects=True, vmem_limit_bytes=40 << 20
        ),
    )(activations[0], cotangent[0], momentum[0], pos, f_right, f_left)
    me = lax.axis_index("rep")
    vown = lax.dynamic_index_in_dim(vall, me, 0, keepdims=False)
    chunk = pl.BlockSpec((128, 1024), lambda i: (i, 0))
    every = pl.BlockSpec((16, 8, 128), lambda i: (0, i, 0))
    mine = pl.BlockSpec((8, 128), lambda i: (i, 0))
    nm, st = pl.pallas_call(
        spread_kernel,
        grid=(4,),
        out_shape=(jax.ShapeDtypeStruct((512, 1024), F32), jax.ShapeDtypeStruct((512, 1024), F32)),
        in_specs=[
            chunk, every, every, mine, mine,
            pl.BlockSpec((512, 256), lambda i: (0, 0)), pl.BlockSpec((128, 384), lambda i: (0, 0)),
        ],
        out_specs=(chunk, chunk),
        scratch_shapes=[pltpu.VMEM((256, 1024), F32)],
        name="spread",
        compiler_params=pltpu.CompilerParams(vmem_limit_bytes=40 << 20),
    )(upd, vall, pall, vown, pos, i_right, i_left)
    return nm[None], st


def solution(mesh):
    return jax.shard_map(
        per_device,
        mesh=mesh,
        in_specs=(
            P("rep", "fsdp", None),
            P("rep", "fsdp", None),
            P("rep", "fsdp", None),
            P("rep", "fsdp", None),
        ),
        out_specs=(P("rep", "fsdp", None), P("fsdp", None)),
        check_vma=False,
    )
```

time: 372 us -> 101 us (0.27)
  the two profiles are of different devices: /device:TPU:2 before, /device:TPU:1 now
where the time goes in v1:
time: 101 us; the launch traced here: 100 us
  Pallas kernels  92.8 us (92%)
  local copies, waits for them, and re-layouts  6.88 us (7%)
    pallas_call x1, Pallas kernels, per_device(): pl.pallas_call(gather_kernel, out_shape=(jax.ShapeDtypeStruct((512, 1024)...  65.5 us
    pallas_call x1, Pallas kernels, per_device(): pl.pallas_call(spread_kernel, grid=(4,), out_shape=(jax.ShapeDtypeStruct(...  27.3 us
    unnamed x15, local copies, waits for them, and re-layouts  6.79 us

profile of v1, /device:TPU:1, one launch (start us, length us, event | category | flops | bytes accessed | tf_op | source)
XLA Modules:
  0.0 100.3 jit_solution(3120352317465065499)
XLA Ops:
  0.6 0.8 copy.11
  1.4 0.1 reshape.7.pos.pown
  1.5 0.0 copy-start
  1.5 1.6 %copy-done = bf16[1,128,8192]{2,1,0:T(8,128)(2,1)S(1)} copy-done((bf16[1,128,8192]{2,1,0:T(8,128)(2,1)S(1)}, bf16[1,128,8192]{2,1,0:T(8,128)(2,1)}, u32[]{:S(2)}) %copy-start) | copy-done | bytes 2097176
  3.1 0.0 copy-start.1
  3.1 1.6 %copy-done.1 = f32[1,512,1024]{2,1,0:T(8,128)S(1)} copy-done((f32[1,512,1024]{2,1,0:T(8,128)S(1)}, f32[1,512,1024]{2,1,0:T(8,128)}, u32[]{:S(2)}) %copy-start.1) | copy-done | bytes 2097176
  4.7 0.0 copy-start.2
  4.7 0.9 copy-done.2
  5.7 0.0 copy-start.4
  5.7 0.9 copy-done.4
  6.6 0.0 copy-start.6
  6.6 0.9 copy-done.6
  7.5 0.0 copy-start.3
  7.5 0.0 copy-start.5
  7.5 65.5 %gather.1 = (f32[512,1024]{1,0:T(8,128)S(1)}, f32[16,32,128]{2,1,0:T(8,128)S(1)}, s32[16,32,128]{2,1,0:T(8,128)S(1)}) custom-call(bf16[128,8192]{1,0:T(8,128)(2,1)S(1)} %bitcast.6, bf16[128,1024]{1,0:T(8,128)(2,1)S(1)} %bitcast.8, f32[512,1024]{1,0:T(8,128)S(1)} %bitcast.7, s32[32,128]{1,0:T(8,128)S(1)} %reshape.7.pos.pown, bf16[512,256]{1,0:T(8,128)(2,1)S(1)} %copy-done.4, ...), custom_call_target="tpu_custom_call" | custom-call | tf_op jit(solution)/shard_map/gather/pallas_call | solution.py:305
  73.0 0.0 copy-done.3
  73.0 0.0 copy-done.5
  73.0 27.3 %spread.1 = (f32[512,1024]{1,0:T(8,128)}, f32[512,1024]{1,0:T(8,128)}) custom-call(f32[512,1024]{1,0:T(8,128)S(1)} %get-tuple-element.7.upd, f32[16,32,128]{2,1,0:T(8,128)S(1)} %get-tuple-element.8.vall, s32[16,32,128]{2,1,0:T(8,128)S(1)} %get-tuple-element.9.pall, f32[32,128]{1,0:T(8,128)S(1)} %dynamic-slice_bitcast_fusion.vown, ...), custom_call_target="tpu_custom_call" | custom-call | tf_op jit(solution)/shard_map/spread/pallas_call | solution.py:333
  (1 shorter events, 0.0 us)
Async XLA Ops:
  1.5 1.6 %copy-start = (bf16[1,128,8192]{2,1,0:T(8,128)(2,1)S(1)}, bf16[1,128,8192]{2,1,0:T(8,128)(2,1)}, u32[]{:S(2)}) copy-start(bf16[1,128,8192]{2,1,0:T(8,128)(2,1)} %param.8) | copy-start | bytes 6291460
  3.1 1.6 %copy-start.1 = (f32[1,512,1024]{2,1,0:T(8,128)S(1)}, f32[1,512,1024]{2,1,0:T(8,128)}, u32[]{:S(2)}) copy-start(f32[1,512,1024]{2,1,0:T(8,128)} %param.10) | copy-start | bytes 6291460
  4.7 0.9 copy-start.2
  5.7 0.9 copy-start.4
  6.6 0.9 copy-start.6
  7.5 65.5 %copy-start.3 = (bf16[512,256]{1,0:T(8,128)(2,1)S(1)}, bf16[512,256]{1,0:T(8,128)(2,1)}, u32[]{:S(2)}) copy-start(bf16[512,256]{1,0:T(8,128)(2,1)} %constant.21.clone.rtab) | copy-start | bytes 786436
  7.5 65.5 %copy-start.5 = (bf16[128,384]{1,0:T(8,128)(2,1)S(1)}, bf16[128,384]{1,0:T(8,128)(2,1)}, u32[]{:S(2)}) copy-start(bf16[128,384]{1,0:T(8,128)(2,1)} %constant.22.clone.ltab) | copy-start | bytes 294916

commit v2 on v0

v2 whole, which is shorter than its diff:
```python
import functools

import jax
import jax.numpy as jnp
import numpy as np
from jax import lax
from jax.experimental import pallas as pl
from jax.experimental.pallas import tpu as pltpu
from jax.sharding import PartitionSpec as P

GROUP = 64
MESH = pl.DeviceIdType.MESH
BF = jnp.bfloat16
F32 = jnp.float32
LAG = 2
NEAR = ((1, 0), (3, 0), (2, 0), (1, 1), (3, 1), (2, 1), (0, 1))


def dot(a, b):
    return jnp.dot(a, b, preferred_element_type=F32)


def split(x):
    hi = x.astype(BF)
    return hi, (x - hi.astype(F32)).astype(BF)


def right_mul(x, table_ref):
    m = x.shape[0]
    hi, lo = split(x)
    both = dot(jnp.concatenate([hi, lo], 0), table_ref[0:256, :])
    return both[:m] + both[m:] + dot(hi, table_ref[256:512, :])


def left_mul(table_ref, y):
    hi, lo = split(y)
    return dot(table_ref[...], jnp.concatenate([hi, hi, lo], 0))


def fill_tables(rt, lt):
    k = lax.broadcasted_iota(jnp.int32, (256, 256), 0)
    n = lax.broadcasted_iota(jnp.int32, (256, 256), 1)
    phase = ((2 * (n & 63) + 1) * (k & 63)) & 255
    scale = jnp.where((k & 63) == 0, 0.125, (2.0 / GROUP) ** 0.5)
    table = jnp.cos(phase.astype(F32) * (np.pi / 128)) * scale
    table = jnp.where((k >> 6) == (n >> 6), table, 0.0)
    turned = table.T
    for i, (left, right) in enumerate(((table, turned), (turned, table))):
        hi, lo = split(right)
        rt[i] = jnp.concatenate([hi, lo], 0)
        hi, lo = split(left[0:128, 0:128])
        lt[i] = jnp.concatenate([hi, lo, hi], 1)


def dot_t(a, b):
    return lax.dot_general(a, b, (((1,), (1,)), ((), ())), preferred_element_type=F32)


def t_dot(a, b):
    return lax.dot_general(a, b, (((0,), (0,)), ((), ())), preferred_element_type=F32)


def transform(x_ref, rows, rtab, ltab):
    half = [right_mul(x_ref[rows, q * 256 : q * 256 + 256], rtab) for q in range(4)]
    return [left_mul(ltab, h) for h in half]


def one_hot(iota, row):
    return jnp.where(iota == row, 1.0, 0.0).astype(BF)


def step_kernel(
    act, cot, mom, pos,
    nm, st,
    abuf, cbuf, xsend, xrecv, mbuf, pall, vall, prow, turned, orow, wide, kept, low_hot, high_hot, vrow, dense, rt, lt,
    c_send, c_recv, f_send, f_recv, a_send, a_recv, x_send, x_recv,
    p_send, p_recv, v_send, v_recv, local,
):
    f = lax.axis_index("fsdp")
    r = lax.axis_index("rep")
    xh, y, c = f // 8, (f // 2) % 4, f % 2
    slot = y * 2 + c

    def near(dy, dc):
        return (y + dy) % 4, (c + dc) % 2

    def fs(xx, yy, cc):
        return {"fsdp": xx * 8 + yy * 2 + cc}

    def block(s, n=128):
        return pl.ds(pl.multiple_of(s * n, n), n)

    def quarter(h):
        return pl.ds(h * 256, 256)

    def remote(src, dst, send, recv, device):
        return pltpu.make_async_remote_copy(
            src_ref=src, dst_ref=dst, send_sem=send, recv_sem=recv,
            device_id=device, device_id_type=MESH,
        )

    mate = fs(xh, y, 1 - c)
    over = fs(1 - xh, y, c)

    def rep(d):
        return {"rep": (r + d) % 16}

    def columns(s, j):
        xx = jnp.where(j < 4, 1 - xh, xh)
        return pl.ds(pl.multiple_of((xx * 8 + s) * 512 + (j % 4) * 128, 128), 128)

    own_act = [
        pltpu.make_async_copy(
            act.at[:, pl.ds(pl.multiple_of((xx * 8 + slot) * 512, 512), 512)],
            abuf.at[block(slot), pl.ds(k * 512, 512)], local.at[k],
        )
        for k, xx in enumerate((1 - xh, xh))
    ]
    own_cot = pltpu.make_async_copy(cot, cbuf.at[block(slot)], local.at[2])
    own_pos = pltpu.make_async_copy(pos, pall.at[block(r, 32)], local.at[3])
    get_mom = pltpu.make_async_copy(mom, mbuf, local.at[4])
    own_pos.start()

    barrier = pltpu.get_barrier_semaphore()
    for dy, dc in NEAR:
        pl.semaphore_signal(barrier, inc=1, device_id=fs(xh, *near(dy, dc)), device_id_type=MESH)
    pl.semaphore_signal(barrier, inc=1, device_id=over, device_id_type=MESH)
    for d in range(1, 16):
        pl.semaphore_signal(barrier, inc=1, device_id=rep(d), device_id_type=MESH)
    own_cot.start()
    for copy in own_act:
        copy.start()
    pl.semaphore_wait(barrier, 23)

    with_mate = tuple(enumerate(NEAR[:3] + NEAR[6:]))

    def cot_send(i, dy, dc, h):
        return remote(
            cot.at[:, quarter(h)], cbuf.at[block(slot), quarter(h)], c_send.at[i, h], c_recv.at[i, h],
            fs(xh, *near(dy, dc)),
        )

    def cot_arrival(i, dy, dc, h):
        yy, cc = near(4 - dy, dc)
        place = cbuf.at[block(yy * 2 + cc), quarter(h)]
        return remote(place, place, c_send.at[i, h], c_recv.at[i, h], mate)

    def cot_forward(i, h, cc):
        yy = (y + 4 - NEAR[i][0]) % 4
        place = cbuf.at[block(yy * 2 + cc), quarter(h)]
        return remote(place, place, f_send.at[i, h], f_recv.at[i, h], mate)

    def act_send(i, dy, dc, j):
        yy, cc = near(dy, dc)
        return remote(
            act.at[:, columns(yy * 2 + cc, j)], abuf.at[block(slot), block(j)],
            a_send.at[i, j], a_recv.at[i, j], fs(xh, yy, cc),
        )

    def act_arrival(i, dy, dc, j):
        yy, cc = near(4 - dy, dc)
        place = abuf.at[block(yy * 2 + cc), block(j)]
        return remote(place, place, a_send.at[i, j], a_recv.at[i, j], mate)

    def part_send(u, h):
        rows = block(u)
        return remote(
            xsend.at[rows, quarter(h)], xrecv.at[rows, quarter(h)], x_send.at[u, h], x_recv.at[u, h], over
        )

    def pos_send(d, source):
        return remote(
            pos, pall.at[block(source, 32)], p_send.at[d - 1], p_recv.at[d - 1], rep(d)
        )

    def val_send(d, j, source):
        place = vall.at[source, block(j, 8)]
        return remote(place, place, v_send.at[d - 1, j], v_recv.at[d - 1, j], rep(d))

    def send_acts(j, carry=0):
        for i, (dy, dc) in enumerate(NEAR):
            act_send(i, dy, dc, j).start()
        return carry

    for h in range(4):
        for i, (dy, dc) in with_mate:
            cot_send(i, dy, dc, h).start()
        send_acts(h)
        if h == 0:
            for d in range(1, 16):
                pos_send(d, r).start()
    lax.fori_loop(4, 8, send_acts, 0)
    get_mom.start()

    fill_tables(rt, lt)
    own_pos.wait()
    mine = pall[block(r, 32), :]
    turned[...] = jnp.concatenate([mine] * 4, 0).T
    lane_group = lax.broadcasted_iota(jnp.int32, (32, 128), 1) // 32
    rows32 = turned[pl.ds(0, 32, stride=4), :]
    for q in range(1, 4):
        rows32 = jnp.where(lane_group == q, turned[pl.ds(q, 32, stride=4), :], rows32)
    orow[...] = rows32
    lane1 = lax.broadcasted_iota(jnp.int32, (1, 128), 1) // 32 * 64
    iota256 = lax.broadcasted_iota(jnp.int32, (256, 128), 0)
    iota64 = lax.broadcasted_iota(jnp.int32, (64, 128), 0)

    def own_masks(p, carry):
        for q in range(4):
            t = p * 4 + q
            row = orow[pl.ds(t, 1), :]
            spread = one_hot(iota256, (row & 63) + lane1)
            wide[t] = spread
            kept[block(p, 64), q * 256 : q * 256 + 256] = dot_t(one_hot(iota64, row >> 6), spread).astype(BF)
        return carry

    lax.fori_loop(0, 8, own_masks, 0)

    def gather_rows():
        for d in range(1, 16):
            pos_send(d, (r + 16 - d) % 16).wait_recv()
        for k in range(4):
            prow[:, k * 128 : k * 128 + 128] = pall[k * 128 : k * 128 + 128, :].T

    iota512 = lax.broadcasted_iota(jnp.int32, (64, 512), 0).astype(jnp.int16)

    def all_masks(h):
        def group(g, carry):
            row = prow[pl.ds(g, 1), :]
            for part, out in ((row & 63, low_hot), (row >> 6, high_hot)):
                part = jnp.broadcast_to(part.astype(jnp.int16), (64, 512))
                out[g] = jnp.where(iota512 == part, jnp.ones((), BF), jnp.zeros((), BF))
            return carry

        lax.fori_loop(h * 32, h * 32 + 32, group, 0)

    def wait_acts(j):
        for i, (dy, dc) in enumerate(NEAR):
            act_arrival(i, dy, dc, j).wait_recv()

    for h in range(4):
        for i, (dy, dc) in with_mate:
            cot_arrival(i, dy, dc, h).wait_recv()
            if i < 3:
                cot_forward(i, h, c).start()
        for i in range(3):
            cot_forward(i, h, 1 - c).wait_recv()
        if h == 0:
            own_cot.wait()
            own_act[0].wait()
        else:
            done = 128 * h
            xsend[0:done, quarter(h)] = t_dot(abuf[:, 0:done], cbuf[:, quarter(h)]).astype(BF)
            for u in range(h):
                part_send(u, h).start()
        wait_acts(h)
        upto = 256 * (h + 1)
        xsend[block(h), 0:upto] = t_dot(abuf[:, block(h)], cbuf[:, 0:upto]).astype(BF)
        for k in range(h + 1):
            part_send(h, k).start()
        if h == 0:
            gather_rows()
        all_masks(h)

    get_mom.wait()
    own_act[1].wait()

    def momentum(j):
        rows = block(j)
        wait_acts(j + 4)
        grad = t_dot(abuf[:, block(j + 4)], cbuf[...])
        for h in range(4):
            part_send(j, h).wait_recv()
        nm[rows, :] = 0.999 * mbuf[rows, :] + (grad + xrecv[rows, :].astype(F32))
        coeffs = transform(nm, rows, rt.at[0], lt.at[0])
        for q in range(4):
            cols = pl.ds(q * 256, 256)
            dense[:, cols] = coeffs[q] * kept[rows, cols].astype(F32)
            for p in range(2):
                t = j * 8 + p * 4 + q
                hi, lo = split(coeffs[q][p * 64 : p * 64 + 64])
                both = dot(jnp.concatenate([hi, lo], 0), wide[t])
                high = iota64 == (orow[pl.ds(t, 1), :] >> 6)
                picked = jnp.where(high, both[:64] + both[64:], 0.0)
                vall[r, pl.ds(t, 1), :] = jnp.sum(picked, axis=0, keepdims=True)
        for d in range(1, 16):
            val_send(d, j, r).start()
        for q, own in enumerate(transform(dense, pl.ds(0, 128), rt.at[1], lt.at[1])):
            cols = pl.ds(q * 256, 256)
            nm[rows, cols] = nm[rows, cols] - own

    lane8 = lax.broadcasted_iota(jnp.int32, (8, 128), 1) // 32

    def update(j):
        for d in range(1, 16):
            val_send(d, j, (r + 16 - d) % 16).wait_recv()
        for k in range(4):
            tiles = [vall[4 * k + b, block(j, 8), :] for b in range(4)]
            for q in range(4):
                merged = None
                for b in range(4):
                    shift = (b - q) * 32 % 128
                    moved = pltpu.roll(tiles[b], shift, 1) if shift else tiles[b]
                    merged = moved if b == 0 else jnp.where(lane8 == b, moved, merged)
                vrow[q, :, k * 128 : k * 128 + 128] = merged
        for t in range(8):
            parts = []
            for q in range(4):
                g = (j * 8 + t) * 4 + q
                val = vrow[q, t : t + 1, :]
                hi = val.astype(BF)
                lo = (val - hi.astype(F32)).astype(BF)
                hot = high_hot[g]
                both = dot_t(jnp.concatenate([hot * hi, hot * lo], 0), low_hot[g])
                parts.append(both[:64] + both[64:])
            row, col = t // 4 * 64, t % 4 * 256
            dense[row : row + 64, col : col + 256] = jnp.concatenate(parts, 1)
        for q, out in enumerate(transform(dense, pl.ds(0, 128), rt.at[1], lt.at[1])):
            st[block(j), q * 256 : q * 256 + 256] = jnp.tanh(4.0 * out)

    def stage(j, carry):
        @pl.when(j < 4)
        def _():
            momentum(j)

        @pl.when(j >= LAG)
        def _():
            update(j - LAG)

        return carry

    lax.fori_loop(0, 4 + LAG, stage, 0)

    for h in range(4):
        for i, (dy, dc) in with_mate:
            cot_send(i, dy, dc, h).wait_send()
        for i in range(3):
            cot_forward(i, h, c).wait_send()
        for u in range(4):
            part_send(u, h).wait_send()
    for d in range(1, 16):
        pos_send(d, r).wait_send()

    def sent(j, carry):
        for i, (dy, dc) in enumerate(NEAR):
            act_send(i, dy, dc, j).wait_send()
            act_send(i, dy, dc, j + 4).wait_send()
        for d in range(1, 16):
            val_send(d, j, r).wait_send()
        return carry

    lax.fori_loop(0, 4, sent, 0)


def store_kernel(a, b, a_out, b_out, sems):
    copies = [pltpu.make_async_copy(a, a_out, sems.at[0]), pltpu.make_async_copy(b, b_out, sems.at[1])]
    for copy in copies:
        copy.start()
    for copy in copies:
        copy.wait()


def per_device(activations, cotangent, momentum, positions):
    vmem = pl.BlockSpec(memory_space=pltpu.VMEM)
    hbm = pl.BlockSpec(memory_space=pltpu.HBM)
    dma = pltpu.SemaphoreType.DMA
    rows = jax.ShapeDtypeStruct((512, 1024), F32)
    nm, st = pl.pallas_call(
        step_kernel,
        out_shape=(rows, rows),
        in_specs=[hbm] * 4,
        out_specs=(vmem, vmem),
        scratch_shapes=[
            pltpu.VMEM((1024, 1024), BF),
            pltpu.VMEM((1024, 1024), BF),
            pltpu.VMEM((512, 1024), BF),
            pltpu.VMEM((512, 1024), BF),
            pltpu.VMEM((512, 1024), F32),
            pltpu.VMEM((512, 128), jnp.int32),
            pltpu.VMEM((16, 32, 128), F32),
            pltpu.VMEM((128, 512), jnp.int32),
            pltpu.VMEM((128, 128), jnp.int32),
            pltpu.VMEM((32, 128), jnp.int32),
            pltpu.VMEM((32, 256, 128), BF),
            pltpu.VMEM((512, 1024), BF),
            pltpu.VMEM((128, 64, 512), BF),
            pltpu.VMEM((128, 64, 512), BF),
            pltpu.VMEM((4, 8, 512), F32),
            pltpu.VMEM((128, 1024), F32),
            pltpu.VMEM((2, 512, 256), BF),
            pltpu.VMEM((2, 128, 384), BF),
            dma((4, 4)), dma((4, 4)), dma((3, 4)), dma((3, 4)), dma((7, 8)), dma((7, 8)), dma((4, 4)), dma((4, 4)),
            dma((15,)), dma((15,)), dma((15, 4)), dma((15, 4)), dma((5,)),
        ],
        name="step",
        compiler_params=pltpu.CompilerParams(
            collective_id=0, has_side_effects=True, vmem_limit_bytes=48 << 20
        ),
    )(activations[0], cotangent[0], momentum[0], positions[0].T)
    nm, st = pl.pallas_call(
        store_kernel,
        out_shape=(rows, rows),
        in_specs=[vmem, vmem],
        out_specs=(hbm, hbm),
        scratch_shapes=[dma((2,))],
        name="store",
        compiler_params=pltpu.CompilerParams(vmem_limit_bytes=1 << 20),
    )(nm, st)
    return nm[None], st


def solution(mesh):
    return jax.shard_map(
        per_device,
        mesh=mesh,
        in_specs=(
            P("rep", "fsdp", None),
            P("rep", "fsdp", None),
            P("rep", "fsdp", None),
            P("rep", "fsdp", None),
        ),
        out_specs=(P("rep", "fsdp", None), P("fsdp", None)),
        check_vma=False,
    )
```

time: 372 us -> 67.1 us (0.18)
  the two profiles are of different devices: /device:TPU:2 before, /device:TPU:1 now
where the time goes in v2:
time: 67.1 us; the launch traced here: 66.9 us
  Pallas kernels  64.6 us (96%)
  local copies, waits for them, and re-layouts  1.66 us (2%)
    pallas_call x1, Pallas kernels, per_device(): pl.pallas_call(step_kernel, out_shape=(rows, rows), in_specs=[hbm] * 4, o...  62.6 us
    pallas_call x1, Pallas kernels, per_device(): pl.pallas_call(store_kernel, out_shape=(rows, rows), in_specs=[vmem, vmem...  2.03 us
    unnamed x4, local copies, waits for them, and re-layouts  1.66 us

profile of v2, /device:TPU:1, one launch (start us, length us, event | category | flops | bytes accessed | tf_op | source)
XLA Modules:
  0.0 66.9 jit_solution(4588417291164203110)
XLA Ops:
  0.6 0.0 copy-start
  0.6 0.9 %copy-done = bf16[1,128,1024]{2,1,0:T(8,128)(2,1)S(1)} copy-done((bf16[1,128,1024]{2,1,0:T(8,128)(2,1)S(1)}, bf16[1,128,1024]{2,1,0:T(8,128)(2,1)}, u32[]{:S(2)}) %copy-start) | copy-done | bytes 262168
  1.6 0.0 copy-start.1
  1.6 0.7 %copy-done.1 = s32[1,128,32]{1,2,0:T(8,128)S(1)} copy-done((s32[1,128,32]{1,2,0:T(8,128)S(1)}, s32[1,128,32]{1,2,0:T(8,128)}, u32[]{:S(2)}) %copy-start.1) | copy-done | bytes 16408
  2.3 62.6 %step.1 = (f32[512,1024]{1,0:T(8,128)S(1)}, f32[512,1024]{1,0:T(8,128)S(1)}) custom-call(bf16[128,8192]{1,0:T(8,128)(2,1)} %bitcast.9, bf16[128,1024]{1,0:T(8,128)(2,1)S(1)} %bitcast.7, f32[512,1024]{1,0:T(8,128)} %bitcast.10, s32[32,128]{1,0:T(8,128)S(1)} %bitcast.8), custom_call_target="tpu_custom_call" | custom-call | tf_op jit(solution)/shard_map/step/pallas_call | solution.py:368
  64.9 2.0 %store.1 = (f32[512,1024]{1,0:T(8,128)}, f32[512,1024]{1,0:T(8,128)}) custom-call(f32[512,1024]{1,0:T(8,128)S(1)} %get-tuple-element.6.a, f32[512,1024]{1,0:T(8,128)S(1)} %get-tuple-element.7.b), custom_call_target="tpu_custom_call" | custom-call | tf_op jit(solution)/shard_map/store/pallas_call | solution.py:400
Async XLA Ops:
  0.6 1.0 %copy-start = (bf16[1,128,1024]{2,1,0:T(8,128)(2,1)S(1)}, bf16[1,128,1024]{2,1,0:T(8,128)(2,1)}, u32[]{:S(2)}) copy-start(bf16[1,128,1024]{2,1,0:T(8,128)(2,1)} %param.5) | copy-start | bytes 786436
  1.6 0.7 %copy-start.1 = (s32[1,128,32]{1,2,0:T(8,128)S(1)}, s32[1,128,32]{1,2,0:T(8,128)}, u32[]{:S(2)}) copy-start(s32[1,128,32]{1,2,0:T(8,128)} %param.7) | copy-start | bytes 49156

commit v3 on v2

--- a/solution.py
+++ b/solution.py
@@ -13,7 +13,8 @@
 BF = jnp.bfloat16
 F32 = jnp.float32
 LAG = 2
-NEAR = ((1, 0), (3, 0), (2, 0), (1, 1), (3, 1), (2, 1), (0, 1))
+NEAR = ((2, 0), (1, 0), (3, 0), (2, 1), (1, 1), (3, 1), (0, 1))
+FAR_FIRST = (12, 4, 11, 13, 3, 5, 10, 14, 2, 6, 9, 15, 1, 7, 8)
 
 
 def dot(a, b):
@@ -185,14 +186,15 @@
     for h in range(4):
         for i, (dy, dc) in with_mate:
             cot_send(i, dy, dc, h).start()
+        if h == 3:
+            send_acts(4)
         send_acts(h)
         if h == 0:
             for d in range(1, 16):
                 pos_send(d, r).start()
-    lax.fori_loop(4, 8, send_acts, 0)
+    lax.fori_loop(5, 8, send_acts, 0)
     get_mom.start()
 
-    fill_tables(rt, lt)
     own_pos.wait()
     mine = pall[block(r, 32), :]
     turned[...] = jnp.concatenate([mine] * 4, 0).T
@@ -214,8 +216,6 @@
             kept[block(p, 64), q * 256 : q * 256 + 256] = dot_t(one_hot(iota64, row >> 6), spread).astype(BF)
         return carry
 
-    lax.fori_loop(0, 8, own_masks, 0)
-
     def gather_rows():
         for d in range(1, 16):
             pos_send(d, (r + 16 - d) % 16).wait_recv()
@@ -224,7 +224,7 @@
 
     iota512 = lax.broadcasted_iota(jnp.int32, (64, 512), 0).astype(jnp.int16)
 
-    def all_masks(h):
+    def all_masks(first):
         def group(g, carry):
             row = prow[pl.ds(g, 1), :]
             for part, out in ((row & 63, low_hot), (row >> 6, high_hot)):
@@ -232,7 +232,7 @@
                 out[g] = jnp.where(iota512 == part, jnp.ones((), BF), jnp.zeros((), BF))
             return carry
 
-        lax.fori_loop(h * 32, h * 32 + 32, group, 0)
+        lax.fori_loop(first, first + 64, group, 0)
 
     def wait_acts(j):
         for i, (dy, dc) in enumerate(NEAR):
@@ -259,8 +259,13 @@
         for k in range(h + 1):
             part_send(h, k).start()
         if h == 0:
+            fill_tables(rt, lt)
+            lax.fori_loop(0, 8, own_masks, 0)
+        elif h == 1:
             gather_rows()
-        all_masks(h)
+            all_masks(0)
+        elif h == 2:
+            all_masks(64)
 
     get_mom.wait()
     own_act[1].wait()
@@ -283,7 +288,7 @@
                 high = iota64 == (orow[pl.ds(t, 1), :] >> 6)
                 picked = jnp.where(high, both[:64] + both[64:], 0.0)
                 vall[r, pl.ds(t, 1), :] = jnp.sum(picked, axis=0, keepdims=True)
-        for d in range(1, 16):
+        for d in FAR_FIRST:
             val_send(d, j, r).start()
         for q, own in enumerate(transform(dense, pl.ds(0, 128), rt.at[1], lt.at[1])):
             cols = pl.ds(q * 256, 256)
@@ -318,6 +323,32 @@
         for q, out in enumerate(transform(dense, pl.ds(0, 128), rt.at[1], lt.at[1])):
             st[block(j), q * 256 : q * 256 + 256] = jnp.tanh(4.0 * out)
 
+    def all_sent():
+        for h in range(4):
+            for i, (dy, dc) in with_mate:
+                cot_send(i, dy, dc, h).wait_send()
+            for i in range(3):
+                cot_forward(i, h, c).wait_send()
+        for d in range(1, 16):
+            pos_send(d, r).wait_send()
+
+        def sent(j, carry):
+            for i, (dy, dc) in enumerate(NEAR):
+                act_send(i, dy, dc, j).wait_send()
+                act_send(i, dy, dc, j + 4).wait_send()
+            for h in range(4):
+                part_send(j, h).wait_send()
+            return carry
+
+        lax.fori_loop(0, 4, sent, 0)
+
+        def values_sent(j, carry):
+            for d in range(1, 16):
+                val_send(d, j, r).wait_send()
+            return carry
+
+        lax.fori_loop(0, 3, values_sent, 0)
+
     def stage(j, carry):
         @pl.when(j < 4)
         def _():
@@ -327,33 +358,24 @@
         def _():
             update(j - LAG)
 
+        @pl.when(j == 4)
+        def _():
+            all_sent()
+
         return carry
 
     lax.fori_loop(0, 4 + LAG, stage, 0)
 
-    for h in range(4):
-        for i, (dy, dc) in with_mate:
-            cot_send(i, dy, dc, h).wait_send()
-        for i in range(3):
-            cot_forward(i, h, c).wait_send()
-        for u in range(4):
-            part_send(u, h).wait_send()
     for d in range(1, 16):
-        pos_send(d, r).wait_send()
-
-    def sent(j, carry):
-        for i, (dy, dc) in enumerate(NEAR):
-            act_send(i, dy, dc, j).wait_send()
-            act_send(i, dy, dc, j + 4).wait_send()
-        for d in range(1, 16):
-            val_send(d, j, r).wait_send()
-        return carry
-
-    lax.fori_loop(0, 4, sent, 0)
+        val_send(d, 3, r).wait_send()
 
 
 def store_kernel(a, b, a_out, b_out, sems):
-    copies = [pltpu.make_async_copy(a, a_out, sems.at[0]), pltpu.make_async_copy(b, b_out, sems.at[1])]
+    copies = [
+        pltpu.make_async_copy(src.at[pl.ds(k * 128, 128)], dst.at[pl.ds(k * 128, 128)], sems.at[i, k])
+        for i, (src, dst) in enumerate(((a, a_out), (b, b_out)))
+        for k in range(4)
+    ]
     for copy in copies:
         copy.start()
     for copy in copies:
@@ -402,7 +424,7 @@
         out_shape=(rows, rows),
         in_specs=[vmem, vmem],
         out_specs=(hbm, hbm),
-        scratch_shapes=[dma((2,))],
+        scratch_shapes=[dma((2, 4))],
         name="store",
         compiler_params=pltpu.CompilerParams(vmem_limit_bytes=1 << 20),
     )(nm, st)

time: 67.1 us -> 66.7 us (level)
  no operation moved by 1% of the time
where the time goes in v3:
time: 66.7 us; the launch traced here: 66.6 us
  Pallas kernels  64.3 us (96%)
  local copies, waits for them, and re-layouts  1.66 us (2%)
    pallas_call x1, Pallas kernels, per_device(): pl.pallas_call(step_kernel, out_shape=(rows, rows), in_specs=[hbm] * 4, o...  62.2 us
    pallas_call x1, Pallas kernels, per_device(): pl.pallas_call(store_kernel, out_shape=(rows, rows), in_specs=[vmem, vmem...  2.07 us
    unnamed x4, local copies, waits for them, and re-layouts  1.66 us

profile of v3, /device:TPU:1, one launch (start us, length us, event | category | flops | bytes accessed | tf_op | source)
XLA Modules:
  0.0 66.6 jit_solution(15065747094925203600)
XLA Ops:
  0.6 0.0 copy-start
  0.6 0.9 %copy-done = bf16[1,128,1024]{2,1,0:T(8,128)(2,1)S(1)} copy-done((bf16[1,128,1024]{2,1,0:T(8,128)(2,1)S(1)}, bf16[1,128,1024]{2,1,0:T(8,128)(2,1)}, u32[]{:S(2)}) %copy-start) | copy-done | bytes 262168
  1.6 0.0 copy-start.1
  1.6 0.7 %copy-done.1 = s32[1,128,32]{1,2,0:T(8,128)S(1)} copy-done((s32[1,128,32]{1,2,0:T(8,128)S(1)}, s32[1,128,32]{1,2,0:T(8,128)}, u32[]{:S(2)}) %copy-start.1) | copy-done | bytes 16408
  2.3 62.2 %step.1 = (f32[512,1024]{1,0:T(8,128)S(1)}, f32[512,1024]{1,0:T(8,128)S(1)}) custom-call(bf16[128,8192]{1,0:T(8,128)(2,1)} %bitcast.9, bf16[128,1024]{1,0:T(8,128)(2,1)S(1)} %bitcast.7, f32[512,1024]{1,0:T(8,128)} %bitcast.10, s32[32,128]{1,0:T(8,128)S(1)} %bitcast.8), custom_call_target="tpu_custom_call" | custom-call | tf_op jit(solution)/shard_map/step/pallas_call | solution.py:390
  64.5 2.1 %store.1 = (f32[512,1024]{1,0:T(8,128)}, f32[512,1024]{1,0:T(8,128)}) custom-call(f32[512,1024]{1,0:T(8,128)S(1)} %get-tuple-element.6.a, f32[512,1024]{1,0:T(8,128)S(1)} %get-tuple-element.7.b), custom_call_target="tpu_custom_call" | custom-call | tf_op jit(solution)/shard_map/store/pallas_call | solution.py:422
Async XLA Ops:
  0.6 1.0 %copy-start = (bf16[1,128,1024]{2,1,0:T(8,128)(2,1)S(1)}, bf16[1,128,1024]{2,1,0:T(8,128)(2,1)}, u32[]{:S(2)}) copy-start(bf16[1,128,1024]{2,1,0:T(8,128)(2,1)} %param.5) | copy-start | bytes 786436
  1.6 0.7 %copy-start.1 = (s32[1,128,32]{1,2,0:T(8,128)S(1)}, s32[1,128,32]{1,2,0:T(8,128)}, u32[]{:S(2)}) copy-start(s32[1,128,32]{1,2,0:T(8,128)} %param.7) | copy-start | bytes 49156

commit v4 on v3

--- a/solution.py
+++ b/solution.py
@@ -239,7 +239,7 @@
             act_arrival(i, dy, dc, j).wait_recv()
 
     for h in range(4):
-        for i, (dy, dc) in with_mate:
+        for i, (dy, dc) in with_mate[1:3] + with_mate[:1] + with_mate[3:]:
             cot_arrival(i, dy, dc, h).wait_recv()
             if i < 3:
                 cot_forward(i, h, c).start()

time: 66.7 us -> 66.7 us (level)
  no operation moved by 1% of the time
where the time goes in v4:
time: 66.7 us; the launch traced here: 66.5 us
  Pallas kernels  64.2 us (96%)
  local copies, waits for them, and re-layouts  1.66 us (2%)
    pallas_call x1, Pallas kernels, per_device(): pl.pallas_call(step_kernel, out_shape=(rows, rows), in_specs=[hbm] * 4, o...  62.2 us
    pallas_call x1, Pallas kernels, per_device(): pl.pallas_call(store_kernel, out_shape=(rows, rows), in_specs=[vmem, vmem...  2.07 us
    unnamed x4, local copies, waits for them, and re-layouts  1.66 us

profile of v4, /device:TPU:1, one launch (start us, length us, event | category | flops | bytes accessed | tf_op | source)
XLA Modules:
  0.0 66.5 jit_solution(3548055236199645689)
XLA Ops:
  0.6 0.0 copy-start
  0.6 0.9 %copy-done = bf16[1,128,1024]{2,1,0:T(8,128)(2,1)S(1)} copy-done((bf16[1,128,1024]{2,1,0:T(8,128)(2,1)S(1)}, bf16[1,128,1024]{2,1,0:T(8,128)(2,1)}, u32[]{:S(2)}) %copy-start) | copy-done | bytes 262168
  1.6 0.0 copy-start.1
  1.6 0.7 %copy-done.1 = s32[1,128,32]{1,2,0:T(8,128)S(1)} copy-done((s32[1,128,32]{1,2,0:T(8,128)S(1)}, s32[1,128,32]{1,2,0:T(8,128)}, u32[]{:S(2)}) %copy-start.1) | copy-done | bytes 16408
  2.3 62.2 %step.1 = (f32[512,1024]{1,0:T(8,128)S(1)}, f32[512,1024]{1,0:T(8,128)S(1)}) custom-call(bf16[128,8192]{1,0:T(8,128)(2,1)} %bitcast.9, bf16[128,1024]{1,0:T(8,128)(2,1)S(1)} %bitcast.7, f32[512,1024]{1,0:T(8,128)} %bitcast.10, s32[32,128]{1,0:T(8,128)S(1)} %bitcast.8), custom_call_target="tpu_custom_call" | custom-call | tf_op jit(solution)/shard_map/step/pallas_call | solution.py:390
  64.5 2.1 %store.1 = (f32[512,1024]{1,0:T(8,128)}, f32[512,1024]{1,0:T(8,128)}) custom-call(f32[512,1024]{1,0:T(8,128)S(1)} %get-tuple-element.6.a, f32[512,1024]{1,0:T(8,128)S(1)} %get-tuple-element.7.b), custom_call_target="tpu_custom_call" | custom-call | tf_op jit(solution)/shard_map/store/pallas_call | solution.py:422
Async XLA Ops:
  0.6 1.0 %copy-start = (bf16[1,128,1024]{2,1,0:T(8,128)(2,1)S(1)}, bf16[1,128,1024]{2,1,0:T(8,128)(2,1)}, u32[]{:S(2)}) copy-start(bf16[1,128,1024]{2,1,0:T(8,128)(2,1)} %param.5) | copy-start | bytes 786436
  1.6 0.7 %copy-start.1 = (s32[1,128,32]{1,2,0:T(8,128)S(1)}, s32[1,128,32]{1,2,0:T(8,128)}, u32[]{:S(2)}) copy-start(s32[1,128,32]{1,2,0:T(8,128)} %param.7) | copy-start | bytes 49156
